TPU v7x, 32 devices: a whole 2x2x4 slice. The times are simulated.
32 devices in a mesh: groups: 2 (over y), expert: 4 (over z), dp: 4 (over x, core).
Axes of the slice: x: 2, y: 2, z: 4, core: 2. Of those that a mesh axis runs over, the one named last changes fastest.
Arguments:
- tokens: bfloat16 [4096, 2048], P(('groups', 'expert', 'dp')), parts along dimension 0, may hold values from -6 to 6
- cotangent: bfloat16 [4096, 2048], P(('groups', 'expert', 'dp')), parts along dimension 0, may hold values from -6 to 6
- expert_ids: int32 [4096, 2], P(('groups', 'expert', 'dp')), parts along dimension 0, may hold values from 0 to 3, as said below
- gate_fix: int32 [4096, 2], P(('groups', 'expert', 'dp')), parts along dimension 0, may hold values from 4096 to 65535
- w_up: bfloat16 [4, 2048, 768], P('expert', 'dp'), may hold values from -0.125 to 0.125
- w_down: bfloat16 [4, 768, 2048], P('expert', None, 'dp'), may hold values from -0.21875 to 0.21875
Outputs:
- mixed: bfloat16 [4096, 2048], P(('groups', 'expert', 'dp')), parts along dimension 0
- grad_tokens: bfloat16 [4096, 2048], P(('groups', 'expert', 'dp')), parts along dimension 0
- grad_up: bfloat16 [8, 2048, 768], P(('groups', 'expert'), 'dp'), parts along dimension 0
- grad_down: bfloat16 [8, 768, 2048], P(('groups', 'expert'), None, 'dp'), parts along dimension 0
There are 2 independent parts, one for each index of `groups`. A program takes and returns all parts, laid end to end along the dimension named above; an argument that names none is the same for every part. Nothing has to cross between parts.
Inputs may be any that keep to these rules, and one draw needn't show every extreme that they name: `expert_ids`: column 0 of row t is its home expert t // (128 * 4); column 1 is the next or the previous expert on the cycle of 4. Among the 128 rows of one device at most 80 name the next expert and at most 80 name the previous one; both bounds are reached by some device in every draw.
All inputs are finite; a program needn't handle non-finite values.
Results may differ from a plain program's by a relative error of at most 0.0065.
Values may be sent and summed in bfloat16 or wider, within the bound.
A program may use at most 64 MiB of HBM per device.

v0:
```python
import jax
import jax.numpy as jnp
from jax import lax
from jax.sharding import PartitionSpec as P

CAP = 80


def from_behind(value, axis, steps):
    count = lax.axis_size(axis)
    pairs = [(source, (source + steps) % count) for source in range(count)]
    return lax.ppermute(value, axis, pairs)


def select_rows(picker, data):
    return jnp.dot(picker, data, preferred_element_type=jnp.float32).astype(jnp.bfloat16)


def spread_rows(picker, data):
    return lax.dot_general(
        picker, data, (((0,), (0,)), ((), ())), preferred_element_type=jnp.float32
    )


def local(tokens, cotangent, expert_ids, gate_fix, w_up, w_down):
    rows, width = tokens.shape
    slots = lax.axis_size("dp")
    cycle = lax.axis_size("expert")
    place = lax.axis_index("expert")
    after = (place + 1) % cycle
    fixed = gate_fix.astype(jnp.float32)
    gates = fixed / jnp.sum(fixed, axis=1, keepdims=True)
    home_gate = gates[:, 0:1]
    side_gate = gates[:, 1:2]
    goes_next = expert_ids[:, 1] == after
    goes_prev = jnp.logical_not(goes_next)
    cot_wide = cotangent.astype(jnp.float32)
    home_scaled = (home_gate * cot_wide).astype(jnp.bfloat16)
    side_scaled = (side_gate * cot_wide).astype(jnp.bfloat16)
    slot_ids = jnp.arange(CAP, dtype=jnp.int32)[:, None]
    slot_next = jnp.cumsum(goes_next.astype(jnp.int32)) - 1
    slot_prev = jnp.cumsum(goes_prev.astype(jnp.int32)) - 1
    pick_next = jnp.logical_and(slot_ids == slot_next[None, :], goes_next[None, :]).astype(
        jnp.bfloat16
    )
    pick_prev = jnp.logical_and(slot_ids == slot_prev[None, :], goes_prev[None, :]).astype(
        jnp.bfloat16
    )
    send_next = (select_rows(pick_next, tokens), select_rows(pick_next, side_scaled))
    send_prev = (select_rows(pick_prev, tokens), select_rows(pick_prev, side_scaled))
    from_prev = from_behind((send_next[0], send_next[1]), "expert", 1)
    from_next = from_behind((send_prev[0], send_prev[1]), "expert", -1)
    visiting = from_prev[0].shape[0]
    rows_in = jnp.concatenate([tokens, from_prev[0], from_next[0]], axis=0)
    scaled = jnp.concatenate([home_scaled, from_prev[1], from_next[1]], axis=0)
    up_full, down_full = (
        lax.all_gather(w_up[0], "dp", axis=0, tiled=True),
        lax.all_gather(w_down[0], "dp", axis=1, tiled=True),
    )
    hidden = jnp.dot(rows_in, up_full, preferred_element_type=jnp.float32)
    sig = 1.0 / (1.0 + jnp.exp(-hidden))
    act = (hidden * sig).astype(jnp.bfloat16)
    expert_out = jnp.dot(act, down_full, preferred_element_type=jnp.float32).astype(jnp.bfloat16)
    out_home = expert_out[:rows]
    out_from_prev = expert_out[rows : rows + visiting]
    out_from_next = expert_out[rows + visiting :]
    back_out_next = from_behind(out_from_prev, "expert", -1)
    back_out_prev = from_behind(out_from_next, "expert", 1)
    d_act = lax.dot_general(
        scaled, down_full, (((1,), (1,)), ((), ())), preferred_element_type=jnp.float32
    )
    d_hidden = (d_act * sig * (1.0 + hidden * (1.0 - sig))).astype(jnp.bfloat16)
    d_in = lax.dot_general(
        d_hidden, up_full, (((1,), (1,)), ((), ())), preferred_element_type=jnp.float32
    ).astype(jnp.bfloat16)
    dx_home = d_in[:rows]
    dx_from_prev = d_in[rows : rows + visiting]
    dx_from_next = d_in[rows + visiting :]
    back_dx_next = from_behind(dx_from_prev, "expert", -1)
    back_dx_prev = from_behind(dx_from_next, "expert", 1)
    total_rows = rows_in.shape[0]
    up_term = lax.dot_general(
        rows_in, d_hidden, (((0,), (0,)), ((), ())), preferred_element_type=jnp.float32
    )
    up_pieces = up_term.astype(jnp.bfloat16).reshape(slots, width // slots, d_hidden.shape[1])
    down_pieces = jnp.einsum(
        "rf,rnk->nfk",
        act,
        scaled.reshape(total_rows, slots, width // slots),
        preferred_element_type=jnp.float32,
    ).astype(jnp.bfloat16)
    got_up, got_down = (
        lax.all_to_all(up_pieces, "dp", split_axis=0, concat_axis=0, tiled=True),
        lax.all_to_all(down_pieces, "dp", split_axis=0, concat_axis=0, tiled=True),
    )
    grad_up = jnp.sum(got_up.astype(jnp.float32), axis=0).astype(jnp.bfloat16)[None]
    grad_down = jnp.sum(got_down.astype(jnp.float32), axis=0).astype(jnp.bfloat16)[None]
    side_out = spread_rows(pick_next, back_out_next) + spread_rows(pick_prev, back_out_prev)
    side_dx = spread_rows(pick_next, back_dx_next) + spread_rows(pick_prev, back_dx_prev)
    mixed = (home_gate * out_home.astype(jnp.float32) + side_gate * side_out).astype(jnp.bfloat16)
    grad_tokens = (dx_home.astype(jnp.float32) + side_dx).astype(jnp.bfloat16)
    return (mixed, grad_tokens, grad_up, grad_down)


def solution(mesh):
    in_specs = (
        P(("groups", "expert", "dp"), None),
        P(("groups", "expert", "dp"), None),
        P(("groups", "expert", "dp"), None),
        P(("groups", "expert", "dp"), None),
        P("expert", "dp", None),
        P("expert", None, "dp"),
    )
    out_specs = (
        P(("groups", "expert", "dp"), None),
        P(("groups", "expert", "dp"), None),
        P(("groups", "expert"), "dp", None),
        P(("groups", "expert"), None, "dp"),
    )
    return jax.shard_map(local, mesh=mesh, in_specs=in_specs, out_specs=out_specs, check_vma=False)
```

profile of v0, /device:TPU:0, one launch (start us, length us, event | category | flops | bytes accessed | tf_op | source)
XLA Modules:
  0.0 159.4 jit_solution(17691349376727149250)
XLA Ops:
  8.0 0.7 all-gather.7.cloned.1.call-update
  9.4 3.1 %collective-permute-start = (bf16[80,2048]{1,0:T(8,128)(2,1)S(1)}, bf16[80,2048]{1,0:T(8,128)(2,1)S(1)}, u32[]{:S(2)}, u32[]{:S(2)}) collective-permute-start(bf16[80,2048]{1,0:T(8,128)(2,1)S(1)} %convolution_convert_fusion.4), channel_id=1, source_target_pairs={{0,4},{4,8},{8,12},{12,0},{1,5},{5,9},{9,13},{13,1},{2,6},{6,10},{... | collective-permute-start | bytes 983048 | tf_op jit(solution)/shard_map/ppermute | solution.py:12
  13.1 2.1 %collective-permute-start.1 = (bf16[80,2048]{1,0:T(8,128)(2,1)S(1)}, bf16[80,2048]{1,0:T(8,128)(2,1)S(1)}, u32[]{:S(2)}, u32[]{:S(2)}) collective-permute-start(bf16[80,2048]{1,0:T(8,128)(2,1)S(1)} %convolution_convert_fusion.3), channel_id=1, source_target_pairs={{0,12},{4,0},{8,4},{12,8},{1,13},{5,1},{9,5},{13,9},{2,14},{6,2},{... | collective-permute-start | bytes 983048 | tf_op jit(solution)/shard_map/ppermute | solution.py:12
  15.6 2.0 %collective-permute-start.5 = (bf16[80,2048]{1,0:T(8,128)(2,1)S(1)}, bf16[80,2048]{1,0:T(8,128)(2,1)S(1)}, u32[]{:S(2)}, u32[]{:S(2)}) collective-permute-start(bf16[80,2048]{1,0:T(8,128)(2,1)S(1)} %convolution_convert_fusion.1), channel_id=1, source_target_pairs={{0,12},{4,0},{8,4},{12,8},{1,13},{5,1},{9,5},{13,9},{2,14},{6,2},{... | collective-permute-start | bytes 983048 | tf_op jit(solution)/shard_map/ppermute | solution.py:12
  18.3 4.8 %collective-permute-done = bf16[80,2048]{1,0:T(8,128)(2,1)S(1)} collective-permute-done((bf16[80,2048]{1,0:T(8,128)(2,1)S(1)}, bf16[80,2048]{1,0:T(8,128)(2,1)S(1)}, u32[]{:S(2)}, u32[]{:S(2)}) %collective-permute-start) | collective-permute-done | bytes 327712 | tf_op jit(solution)/shard_map/ppermute | solution.py:12
  23.1 6.2 %collective-permute-done.1 = bf16[80,2048]{1,0:T(8,128)(2,1)S(1)} collective-permute-done((bf16[80,2048]{1,0:T(8,128)(2,1)S(1)}, bf16[80,2048]{1,0:T(8,128)(2,1)S(1)}, u32[]{:S(2)}, u32[]{:S(2)}) %collective-permute-start.1) | collective-permute-done | bytes 327712 | tf_op jit(solution)/shard_map/ppermute | solution.py:12
  29.4 7.7 %collective-permute-done.5 = bf16[80,2048]{1,0:T(8,128)(2,1)S(1)} collective-permute-done((bf16[80,2048]{1,0:T(8,128)(2,1)S(1)}, bf16[80,2048]{1,0:T(8,128)(2,1)S(1)}, u32[]{:S(2)}, u32[]{:S(2)}) %collective-permute-start.5) | collective-permute-done | bytes 327712 | tf_op jit(solution)/shard_map/ppermute | solution.py:12
  37.0 6.3 %collective-permute-done.4 = bf16[80,2048]{1,0:T(8,128)(2,1)S(1)} collective-permute-done((bf16[80,2048]{1,0:T(8,128)(2,1)S(1)}, bf16[80,2048]{1,0:T(8,128)(2,1)S(1)}, u32[]{:S(2)}, u32[]{:S(2)}) %collective-permute-start.4) | collective-permute-done | bytes 327712 | tf_op jit(solution)/shard_map/ppermute | solution.py:12
  43.5 1.2 copy-done.5
  44.7 3.0 %fusion.6 = f32[288,768]{1,0:T(8,128)S(1)} fusion(bf16[288,2048]{1,0:T(8,128)(2,1)S(1)} %copy-done.5, bf16[1,2048,768]{2,1,0:T(8,128)(2,1)} %all-gather.5.cloned.1.call-done), kind=kOutput, calls=%fused_computation.7 | convolution fusion | flops 905969664 | bytes 5210112 | tf_op jit(solution)/shard_map/dot_general | solution.py:60
  47.7 1.0 copy-done.10
  48.7 3.6 %convert_bitcast_fusion = bf16[4,768,512]{1,2,0:T(8,128)(2,1)} fusion(bf16[36,4,8,512]{3,2,1,0:T(8,128)(2,1)S(1)} %bitcast.50, f32[288,768]{1,0:T(8,128)S(1)} %fusion.6), kind=kOutput, calls=%fused_computation.9 | convolution fusion | flops 908648448 | bytes 5210112 | tf_op jit(solution)/shard_map/rf,rnk->nfk/dot_general | solution.py:86
  52.3 3.7 %all-to-all-start.1 = ((bf16[4,768,512]{1,2,0:T(8,128)(2,1)}), bf16[4,768,512]{1,2,0:T(8,128)(2,1)S(1)}, u32[]{:S(2)}, u32[]{:S(2)}) async-start(bf16[4,768,512]{1,2,0:T(8,128)(2,1)} %convert_bitcast_fusion), calls=%async_computation.1 | async-start | bytes 6291456 | tf_op jit(solution)/shard_map/all_to_all | solution.py:94
  56.0 25.3 %all-gather.7.cloned.1.call-done = bf16[1,768,2048]{2,1,0:T(8,128)(2,1)} async-done(((bf16[1,768,512]{2,1,0:T(8,128)(2,1)}), bf16[1,768,2048]{2,1,0:T(8,128)(2,1)}) %all-gather.7.cloned.1.call-update) | async-done | bytes 3145744 | tf_op jit(solution)/shard_map/all_gather | solution.py:58
  81.3 3.7 %fusion.25 = bf16[288,768]{1,0:T(8,128)(2,1)S(1)} fusion(bf16[1,768,2048]{2,1,0:T(8,128)(2,1)} %all-gather.7.cloned.1.call-done, f32[288,768]{1,0:T(8,128)} %copy-done.10, bf16[80,2048]{1,0:T(8,128)(2,1)S(1)} %collective-permute-done.5, bf16[80,2048]{1,0:T(8,128)(2,1)} %copy-done.3, bf16[128,2048]{1,0:T(8,128)(2,1)} %copy-done.2), kind=kOutput, calls=%fused_computation.27 | convolution fusion | flops 911499264 | bytes 5652480 | tf_op jit(solution)/shard_map/dot_general | solution.py:69
  85.0 3.5 %convolution_convert_fusion = bf16[2048,768]{1,0:T(8,128)(2,1)} fusion(bf16[288,2048]{1,0:T(8,128)(2,1)S(1)} %copy-done.6, bf16[288,768]{1,0:T(8,128)(2,1)S(1)} %fusion.25), kind=kOutput, calls=%fused_computation | convolution fusion | flops 907542528 | bytes 4767744 | tf_op jit(solution)/shard_map/dot_general | solution.py:82
  88.5 2.2 %fusion.11 = bf16[288,2048]{1,0:T(8,128)(2,1)} fusion(bf16[1,768,2048]{2,1,0:T(8,128)(2,1)S(1)} %copy-done.9, f32[288,768]{1,0:T(8,128)S(1)} %copy-done.11), kind=kOutput, calls=%fused_computation.11 | convolution fusion | flops 907665408 | bytes 5210112 | tf_op jit(solution)/shard_map/dot_general | solution.py:63
  90.7 12.4 %all-to-all-done.1 = bf16[4,768,512]{1,2,0:T(8,128)(2,1)S(1)} async-done(((bf16[4,768,512]{1,2,0:T(8,128)(2,1)}), bf16[4,768,512]{1,2,0:T(8,128)(2,1)S(1)}, u32[]{:S(2)}, u32[]{:S(2)}) %all-to-all-start.1) | async-done | bytes 3145760 | tf_op jit(solution)/shard_map/all_to_all | solution.py:94
  103.1 4.7 %all-to-all-start = ((bf16[4,512,768]{2,1,0:T(8,128)(2,1)}), bf16[4,512,768]{2,1,0:T(8,128)(2,1)}, u32[]{:S(2)}, u32[]{:S(2)}) async-start(bf16[4,512,768]{2,1,0:T(8,128)(2,1)} %bitcast.48), calls=%async_computation | async-start | bytes 6291456 | tf_op jit(solution)/shard_map/all_to_all | solution.py:93
  107.8 1.2 fusion.64
  109.0 1.5 collective-permute-start.3
  110.5 3.0 %fusion.8 = bf16[288,2048]{1,0:T(8,128)(2,1)S(1)} fusion(bf16[288,768]{1,0:T(8,128)(2,1)S(1)} %copy-done.13, bf16[1,2048,768]{2,1,0:T(8,128)(2,1)} %all-gather.5.cloned.1.call-done), kind=kOutput, calls=%fused_computation.10 | convolution fusion | flops 906559488 | bytes 4767744 | tf_op jit(solution)/shard_map/dot_general | solution.py:73
  113.6 1.5 collective-permute-start.7
  115.1 2.3 %collective-permute-start.2 = (bf16[80,2048]{1,0:T(8,128)(2,1)S(1)}, bf16[80,2048]{1,0:T(8,128)(2,1)S(1)}, u32[]{:S(2)}, u32[]{:S(2)}) collective-permute-start(bf16[80,2048]{1,0:T(8,128)(2,1)S(1)} %get-tuple-element.12), channel_id=1, source_target_pairs={{0,12},{4,0},{8,4},{12,8},{1,13},{5,1},{9,5},{13,9},{2,14},{6,2},{... | collective-permute-start | bytes 983048 | tf_op jit(solution)/shard_map/ppermute | solution.py:12
  118.0 3.5 %collective-permute-done.3 = bf16[80,2048]{1,0:T(8,128)(2,1)S(1)} collective-permute-done((bf16[80,2048]{1,0:T(8,128)(2,1)S(1)}, bf16[80,2048]{1,0:T(8,128)(2,1)S(1)}, u32[]{:S(2)}, u32[]{:S(2)}) %collective-permute-start.3) | collective-permute-done | bytes 327712 | tf_op jit(solution)/shard_map/ppermute | solution.py:12
  121.8 6.6 %collective-permute-done.7 = bf16[80,2048]{1,0:T(8,128)(2,1)S(1)} collective-permute-done((bf16[80,2048]{1,0:T(8,128)(2,1)S(1)}, bf16[80,2048]{1,0:T(8,128)(2,1)S(1)}, u32[]{:S(2)}, u32[]{:S(2)}) %collective-permute-start.7) | collective-permute-done | bytes 327712 | tf_op jit(solution)/shard_map/ppermute | solution.py:12
  128.7 13.2 %collective-permute-done.6 = bf16[80,2048]{1,0:T(8,128)(2,1)S(1)} collective-permute-done((bf16[80,2048]{1,0:T(8,128)(2,1)S(1)}, bf16[80,2048]{1,0:T(8,128)(2,1)S(1)}, u32[]{:S(2)}, u32[]{:S(2)}) %collective-permute-start.6) | collective-permute-done | bytes 327712 | tf_op jit(solution)/shard_map/ppermute | solution.py:12
  141.9 1.1 fusion.18
  143.1 2.2 %fusion.17 = bf16[128,2048]{1,0:T(8,128)(2,1)} fusion(f32[128,2048]{1,0:T(8,128)S(1)} %fusion.44, bf16[80,2048]{1,0:T(8,128)(2,1)S(1)} %collective-permute-done.2, bf16[288,2048]{1,0:T(8,128)(2,1)} %fusion.11, f32[128]{0:T(128)S(1)} %get-tuple-element.15, f32[128]{0:T(128)S(1)} %get-tuple-element.14, s32[128]{0:T(128)S(1)} %add_reduce_fusion.1, ...), kind=kOutput, calls=%fused_computation.17 | convolution fusion | flops 43536384 | bytes 2426496 | tf_op jit(solution)/shard_map/dot_general | solution.py:20
  145.3 1.5 reduce_sum.35
  146.9 2.3 %copy.19 = bf16[1,768,512]{2,1,0:T(8,128)(2,1)} copy(bf16[1,768,512]{1,2,0:T(8,128)(2,1)} %bitcast.49) | data formatting | bytes 1572864
  149.1 3.4 %reduce_sum.34 = bf16[512,768]{1,0:T(8,128)(2,1)} reduce(bf16[4,512,768]{2,1,0:T(8,128)(2,1)} %all-to-all-done, bf16[]{:T(256)} %constant.34.clone.1), dimensions={0}, to_apply=%region_3.4 | reduce | flops 1179648 | bytes 3932162 | tf_op jit(solution)/shard_map/reduce_sum | solution.py:96
  (57 shorter events, 4.5 us)
Async XLA Ops:
  7.2 1.5 copy-start.8
  7.2 2.0 %copy-start = (bf16[128,2048]{1,0:T(8,128)(2,1)S(1)}, bf16[128,2048]{1,0:T(8,128)(2,1)}, u32[]{:S(2)}) copy-start(bf16[128,2048]{1,0:T(8,128)(2,1)} %param.6) | copy-start | bytes 1572868
  7.2 36.3 %all-gather.5.cloned.1.call-start = ((), (), s32[]{:S(2)}) async-start(), calls=%async_computation.2 | async-start | bytes 3932160 | tf_op jit(solution)/shard_map/all_gather | solution.py:57
  7.9 73.3 %all-gather.7.cloned.1.call-start = ((), (), s32[]{:S(2)}) async-start(), calls=%async_computation.3 | async-start | bytes 3932160 | tf_op jit(solution)/shard_map/all_gather | solution.py:58
  8.7 6.6 %copy-start.7 = (s32[128,2]{0,1:T(2,128)S(1)}, s32[128,2]{0,1:T(2,128)}, u32[]{:S(2)}) copy-start(s32[128,2]{0,1:T(2,128)} %param.9) | copy-start | bytes 3076
  8.7 6.6 %copy-start.1 = (bf16[128,2048]{1,0:T(8,128)(2,1)S(1)}, bf16[128,2048]{1,0:T(8,128)(2,1)}, u32[]{:S(2)}) copy-start(bf16[128,2048]{1,0:T(8,128)(2,1)} %param.7) | copy-start | bytes 1572868
  9.4 13.7 %collective-permute-start = (bf16[80,2048]{1,0:T(8,128)(2,1)S(1)}, bf16[80,2048]{1,0:T(8,128)(2,1)S(1)}, u32[]{:S(2)}, u32[]{:S(2)}) collective-permute-start(bf16[80,2048]{1,0:T(8,128)(2,1)S(1)} %convolution_convert_fusion.4), channel_id=1, source_target_pairs={{0,4},{4,8},{8,12},{12,0},{1,5},{5,9},{9,13},{13,1},{2,6},{6,10},{... | collective-permute-start | bytes 983048 | tf_op jit(solution)/shard_map/ppermute | solution.py:12
  13.1 16.2 %collective-permute-start.1 = (bf16[80,2048]{1,0:T(8,128)(2,1)S(1)}, bf16[80,2048]{1,0:T(8,128)(2,1)S(1)}, u32[]{:S(2)}, u32[]{:S(2)}) collective-permute-start(bf16[80,2048]{1,0:T(8,128)(2,1)S(1)} %convolution_convert_fusion.3), channel_id=1, source_target_pairs={{0,12},{4,0},{8,4},{12,8},{1,13},{5,1},{9,5},{13,9},{2,14},{6,2},{... | collective-permute-start | bytes 983048 | tf_op jit(solution)/shard_map/ppermute | solution.py:12
  15.6 21.4 %collective-permute-start.5 = (bf16[80,2048]{1,0:T(8,128)(2,1)S(1)}, bf16[80,2048]{1,0:T(8,128)(2,1)S(1)}, u32[]{:S(2)}, u32[]{:S(2)}) collective-permute-start(bf16[80,2048]{1,0:T(8,128)(2,1)S(1)} %convolution_convert_fusion.1), channel_id=1, source_target_pairs={{0,12},{4,0},{8,4},{12,8},{1,13},{5,1},{9,5},{13,9},{2,14},{6,2},{... | collective-permute-start | bytes 983048 | tf_op jit(solution)/shard_map/ppermute | solution.py:12
  18.0 25.3 %collective-permute-start.4 = (bf16[80,2048]{1,0:T(8,128)(2,1)S(1)}, bf16[80,2048]{1,0:T(8,128)(2,1)S(1)}, u32[]{:S(2)}, u32[]{:S(2)}) collective-permute-start(bf16[80,2048]{1,0:T(8,128)(2,1)S(1)} %convolution_convert_fusion.2), channel_id=1, source_target_pairs={{0,4},{4,8},{8,12},{12,0},{1,5},{5,9},{9,13},{13,1},{2,6},{6,10},{... | collective-permute-start | bytes 983048 | tf_op jit(solution)/shard_map/ppermute | solution.py:12
  18.2 25.1 %copy-start.2 = (bf16[128,2048]{1,0:T(8,128)(2,1)}, bf16[128,2048]{1,0:T(8,128)(2,1)S(1)}, u32[]{:S(2)}) copy-start(bf16[128,2048]{1,0:T(8,128)(2,1)S(1)} %fusion.30) | copy-start | bytes 1572868
  29.3 7.7 %copy-start.4 = (bf16[288,2048]{1,0:T(8,128)(2,1)}, bf16[288,2048]{1,0:T(8,128)(2,1)S(1)}, u32[]{:S(2)}) copy-start(bf16[288,2048]{1,0:T(8,128)(2,1)S(1)} %constant_dynamic-update-slice_fusion) | copy-start | bytes 3538948
  43.3 4.4 %copy-start.3 = (bf16[80,2048]{1,0:T(8,128)(2,1)}, bf16[80,2048]{1,0:T(8,128)(2,1)S(1)}, u32[]{:S(2)}) copy-start(bf16[80,2048]{1,0:T(8,128)(2,1)S(1)} %collective-permute-done.4) | copy-start | bytes 983044
  43.3 1.4 copy-start.5
  47.7 1.0 copy-start.10
  52.3 50.8 %all-to-all-start.1 = ((bf16[4,768,512]{1,2,0:T(8,128)(2,1)}), bf16[4,768,512]{1,2,0:T(8,128)(2,1)S(1)}, u32[]{:S(2)}, u32[]{:S(2)}) async-start(bf16[4,768,512]{1,2,0:T(8,128)(2,1)} %convert_bitcast_fusion), calls=%async_computation.1 | async-start | bytes 6291456 | tf_op jit(solution)/shard_map/all_to_all | solution.py:94
  81.3 3.7 %copy-start.6 = (bf16[288,2048]{1,0:T(8,128)(2,1)S(1)}, bf16[288,2048]{1,0:T(8,128)(2,1)}, u32[]{:S(2)}) copy-start(bf16[288,2048]{1,0:T(8,128)(2,1)} %copy-done.4) | copy-start | bytes 3538948
  84.9 3.6 %copy-start.12 = (bf16[288,768]{1,0:T(8,128)(2,1)}, bf16[288,768]{1,0:T(8,128)(2,1)S(1)}, u32[]{:S(2)}) copy-start(bf16[288,768]{1,0:T(8,128)(2,1)S(1)} %fusion.25) | copy-start | bytes 1327108
  85.0 3.5 %copy-start.9 = (bf16[1,768,2048]{2,1,0:T(8,128)(2,1)S(1)}, bf16[1,768,2048]{2,1,0:T(8,128)(2,1)}, u32[]{:S(2)}) copy-start(bf16[1,768,2048]{2,1,0:T(8,128)(2,1)} %all-gather.7.cloned.1.call-done) | copy-start | bytes 9437188
  85.0 3.5 %copy-start.11 = (f32[288,768]{1,0:T(8,128)S(1)}, f32[288,768]{1,0:T(8,128)}, u32[]{:S(2)}) copy-start(f32[288,768]{1,0:T(8,128)} %copy-done.10) | copy-start | bytes 2654212
  103.1 46.0 %all-to-all-start = ((bf16[4,512,768]{2,1,0:T(8,128)(2,1)}), bf16[4,512,768]{2,1,0:T(8,128)(2,1)}, u32[]{:S(2)}, u32[]{:S(2)}) async-start(bf16[4,512,768]{2,1,0:T(8,128)(2,1)} %bitcast.48), calls=%async_computation | async-start | bytes 6291456 | tf_op jit(solution)/shard_map/all_to_all | solution.py:93
  107.8 2.7 %copy-start.13 = (bf16[288,768]{1,0:T(8,128)(2,1)S(1)}, bf16[288,768]{1,0:T(8,128)(2,1)}, u32[]{:S(2)}) copy-start(bf16[288,768]{1,0:T(8,128)(2,1)} %copy-done.12) | copy-start | bytes 1327108
  109.0 12.5 %collective-permute-start.3 = (bf16[80,2048]{1,0:T(8,128)(2,1)S(1)}, bf16[80,2048]{1,0:T(8,128)(2,1)S(1)}, u32[]{:S(2)}, u32[]{:S(2)}) collective-permute-start(bf16[80,2048]{1,0:T(8,128)(2,1)S(1)} %get-tuple-element.13), channel_id=1, source_target_pairs={{0,4},{4,8},{8,12},{12,0},{1,5},{5,9},{9,13},{13,1},{2,6},{6,10},{... | collective-permute-start | bytes 983048 | tf_op jit(solution)/shard_map/ppermute | solution.py:12
  113.6 14.8 %collective-permute-start.7 = (bf16[80,2048]{1,0:T(8,128)(2,1)S(1)}, bf16[80,2048]{1,0:T(8,128)(2,1)S(1)}, u32[]{:S(2)}, u32[]{:S(2)}) collective-permute-start(bf16[80,2048]{1,0:T(8,128)(2,1)S(1)} %get-tuple-element.11), channel_id=1, source_target_pairs={{0,4},{4,8},{8,12},{12,0},{1,5},{5,9},{9,13},{13,1},{2,6},{6,10},{... | collective-permute-start | bytes 983048 | tf_op jit(solution)/shard_map/ppermute | solution.py:12
  115.1 28.0 %collective-permute-start.2 = (bf16[80,2048]{1,0:T(8,128)(2,1)S(1)}, bf16[80,2048]{1,0:T(8,128)(2,1)S(1)}, u32[]{:S(2)}, u32[]{:S(2)}) collective-permute-start(bf16[80,2048]{1,0:T(8,128)(2,1)S(1)} %get-tuple-element.12), channel_id=1, source_target_pairs={{0,12},{4,0},{8,4},{12,8},{1,13},{5,1},{9,5},{13,9},{2,14},{6,2},{... | collective-permute-start | bytes 983048 | tf_op jit(solution)/shard_map/ppermute | solution.py:12
  117.5 24.5 %collective-permute-start.6 = (bf16[80,2048]{1,0:T(8,128)(2,1)S(1)}, bf16[80,2048]{1,0:T(8,128)(2,1)S(1)}, u32[]{:S(2)}, u32[]{:S(2)}) collective-permute-start(bf16[80,2048]{1,0:T(8,128)(2,1)S(1)} %get-tuple-element.10), channel_id=1, source_target_pairs={{0,12},{4,0},{8,4},{12,8},{1,13},{5,1},{9,5},{13,9},{2,14},{6,2},{... | collective-permute-start | bytes 983048 | tf_op jit(solution)/shard_map/ppermute | solution.py:12
Sparse Core Ops, SparseCore 0:
  9.6 31.2 all-gather.4
  42.4 38.8 all-gather.6
where the time goes:
time: 160 us; the launch traced here: 159 us
  waiting for transfers between devices  87.3 us (55%)
  matrix products  24.2 us (15%)
  starting transfers between devices  21.7 us (14%)
  between operations  14.3 us (9%)
  local copies, waits for them, and re-layouts  6.11 us (4%)
  other arithmetic  5.83 us (4%)
    ppermute x8, waiting for transfers between devices, from_behind(): return lax.ppermute(value, axis, pairs)  48.2 us
    all_gather x1, waiting for transfers between devices, local(): lax.all_gather(w_down[0], 'dp', axis=1, tiled=True)  25.3 us
    ppermute x8, starting transfers between devices, from_behind(): return lax.ppermute(value, axis, pairs)  13.3 us
    all_to_all x1, waiting for transfers between devices, local(): lax.all_to_all(down_pieces, 'dp', split_axis=0, concat_axis=0, tiled=True)  12.4 us
    all_to_all x1, starting transfers between devices, local(): lax.all_to_all(up_pieces, 'dp', split_axis=0, concat_axis=0, tiled=True)  4.67 us
    unnamed x31, local copies, waits for them, and re-layouts  4.64 us
    dot_general x4, matrix products, spread_rows(): lax.dot_general(picker, data, (((0,), (0,)), ((), ())), preferred_element...  4.05 us
    all_to_all x1, starting transfers between devices, local(): lax.all_to_all(down_pieces, 'dp', split_axis=0, concat_axis=0, tiled=True)  3.7 us
  transfers between devices with their start and end apart: 12, of which 9 were waited for; matrix products, arithmetic and copies ran while one was open for 19% of the time, Pallas kernels for 0%

commit v1 on v0

v1 whole, which is shorter than its diff:
```python
import functools

import jax
import jax.numpy as jnp
from jax import lax
from jax.experimental import pallas as pl
from jax.experimental.pallas import tpu as pltpu
from jax.sharding import PartitionSpec as P

CAP = 80
MESH = pl.DeviceIdType.MESH
F32 = jnp.float32
BF16 = jnp.bfloat16


def nt_dot(left, right):
    return lax.dot_general(left, right, (((1,), (1,)), ((), ())), preferred_element_type=F32)


def tn_dot(left, right):
    return lax.dot_general(left, right, (((0,), (0,)), ((), ())), preferred_element_type=F32)


def dot(left, right):
    return jnp.dot(left, right, preferred_element_type=F32)


def remote(src, dst, sends, recvs, where, device):
    return pltpu.make_async_remote_copy(
        src_ref=src,
        dst_ref=dst,
        send_sem=sends.at[where],
        recv_sem=recvs.at[where],
        device_id=device,
        device_id_type=MESH,
    )


def silu_parts(hidden, d_act):
    sig = 1.0 / (1.0 + jnp.exp(-hidden))
    act = (hidden * sig).astype(BF16)
    d_hidden = (d_act * sig * (1.0 + hidden * (1.0 - sig))).astype(BF16)
    return act, d_hidden


def kernel(
    groups, cycle, slots,
    tok, cot, ids, fix, up_in, down_in,
    mixed, grad_tok, grad_up, grad_down,
    up_w, down_w, pick, home_scl, snd_tok, snd_scl, vis_tok, vis_scl,
    acc_h, acc_d, acc_hv, acc_dv, act_h, dh_h, act_v, dh_v, out_h, din_h,
    ret_out, ret_din, back_out, back_din,
    up_pair, down_pair, up_pair_in, down_pair_in, up_own, down_own,
    up_x, down_x, up_x_in, down_x_in,
    local_sem, pair_s, pair_r, x_s, x_r, y_s, y_r, f_s, f_r, d_s, d_r, r_s, r_r,
    gp_s, gp_r, gx_s, gx_r,
):
    rows = tok.shape[0]
    width = tok.shape[1]
    part = width // slots
    highs = slots // 2
    group = lax.axis_index("groups")
    place = lax.axis_index("expert")
    me = lax.axis_index("dp")
    high = me // 2
    low = me % 2
    other = 1 - low
    pair = high * 2 + other
    after = lax.rem(place + 1, cycle)
    before = lax.rem(place + cycle - 1, cycle)

    def columns(block):
        return pl.ds(pl.multiple_of(block * part, part), part)

    barrier = pltpu.get_barrier_semaphore()
    peers = [{"dp": pair}, {"expert": after}, {"expert": before}]
    peers += [{"dp": lax.rem(high + k, highs) * 2 + low} for k in range(1, highs)]
    peers += [{"groups": lax.rem(group + q, groups)} for q in range(1, groups)]
    for peer in peers:
        pl.semaphore_signal(barrier, inc=1, device_id=peer, device_id_type=MESH)

    goes = jnp.where(ids[:, 1:2] == after, 1.0, 0.0).astype(F32)
    lane = lax.broadcasted_iota(jnp.int32, (rows, rows), 1)
    line = lax.broadcasted_iota(jnp.int32, (rows, rows), 0)
    flags = jnp.where(lane == 0, goes, 1.0 - goes).astype(BF16)
    counts = tn_dot(flags, jnp.where(line <= lane, 1.0, 0.0).astype(BF16))
    marks = tn_dot(flags, jnp.where(line == lane, 1.0, 0.0).astype(BF16))
    slot = lax.broadcasted_iota(jnp.int32, (2 * CAP, rows), 0)
    first = slot < CAP
    wanted = jnp.where(first, slot, slot - CAP).astype(F32) + 1.0
    count = jnp.where(first, counts[0:1, :], counts[1:2, :])
    mark = jnp.where(first, marks[0:1, :], marks[1:2, :])
    pick[...] = jnp.where(count == wanted, mark, 0.0).astype(BF16)
    fixed = fix[...].astype(F32)
    total = fixed[:, 0:1] + fixed[:, 1:2]
    home_gate = fixed[:, 0:1] / total
    side_gate = fixed[:, 1:2] / total

    pl.semaphore_wait(barrier, len(peers))

    weights = ((up_in, up_w), (down_in, down_w))
    local_copies = []
    sends = []
    pair_copies = []
    x_copies = [[], []]
    for w, (own, full) in enumerate(weights):
        half = own.shape[1] // groups
        mine = pl.ds(pl.multiple_of(group * half, half), half)
        for k in range(1, highs):
            copy = remote(
                own.at[0, mine], full.at[me, mine], x_s, x_r, (w, k - 1),
                {"dp": lax.rem(high + k, highs) * 2 + low},
            )
            copy.start()
            x_copies[w].append(copy)
            sends.append(copy)
        copy = remote(own.at[0], full.at[me], pair_s, pair_r, w, {"dp": pair})
        copy.start()
        pair_copies.append(copy)
        sends.append(copy)
        copy = pltpu.make_async_copy(own.at[0], full.at[me], local_sem.at[w])
        copy.start()
        local_copies.append(copy)

    picked = pick[...]
    d_copies = []

    def dispatch(array, src, dst):
        for way, target in enumerate((after, before)):
            span = pl.ds(way * CAP, CAP)
            copy = remote(src.at[span], dst.at[span], d_s, d_r, (array, way), {"expert": target})
            copy.start()
            d_copies.append(copy)
            sends.append(copy)

    snd_tok[...] = dot(picked, tok[...]).astype(BF16)
    dispatch(0, snd_tok, vis_tok)
    wide = cot[...].astype(F32)
    snd_scl[...] = dot(picked, (side_gate * wide).astype(BF16)).astype(BF16)
    dispatch(1, snd_scl, vis_scl)
    home_scl[...] = (home_gate * wide).astype(BF16)

    def add_up(block, first_one, src, acc):
        term = dot(src[:, columns(block)], up_w[block])
        acc[...] = term if first_one else acc[...] + term

    def add_down(block, first_one, src, acc):
        term = nt_dot(src[:, columns(block)], down_w[block])
        acc[...] = term if first_one else acc[...] + term

    adders = ((add_up, tok, acc_h), (add_down, home_scl, acc_d))

    for w, (add, src, acc) in enumerate(adders):
        local_copies[w].wait()
        add(me, True, src, acc)
    for w, (add, src, acc) in enumerate(adders):
        pair_copies[w].wait_recv()
        add(pair, False, src, acc)

    y_copies = {}
    f_copies = {}
    for k in range(1, highs):
        came = lax.rem(high + highs - k, highs) * 2 + low
        for w, (own, full) in enumerate(weights):
            half = own.shape[1] // groups
            mine = pl.ds(pl.multiple_of(group * half, half), half)
            x_copies[w][k - 1].wait_recv()
            piece = full.at[came, mine]
            for q in range(1, groups):
                copy = remote(
                    piece, piece, y_s, y_r, (w, k - 1, q - 1), {"groups": lax.rem(group + q, groups)}
                )
                copy.start()
                y_copies[w, k, q] = copy
                sends.append(copy)
            copy = remote(piece, piece, f_s, f_r, (w, k - 1, 0), {"dp": pair})
            copy.start()
            f_copies[w, k, 0] = copy
            sends.append(copy)
    for k in range(1, highs):
        came = lax.rem(high + highs - k, highs) * 2 + low
        for w, (own, full) in enumerate(weights):
            half = own.shape[1] // groups
            for q in range(1, groups):
                y_copies[w, k, q].wait_recv()
                theirs = lax.rem(group + groups - q, groups)
                piece = full.at[came, pl.ds(pl.multiple_of(theirs * half, half), half)]
                copy = remote(piece, piece, f_s, f_r, (w, k - 1, q), {"dp": pair})
                copy.start()
                f_copies[w, k, q] = copy
                sends.append(copy)
            add, src, acc = adders[w]
            add(came, False, src, acc)
    for k in range(1, highs):
        came = lax.rem(high + highs - k, highs) * 2 + other
        for w in range(2):
            for q in range(groups):
                f_copies[w, k, q].wait_recv()
            add, src, acc = adders[w]
            add(came, False, src, acc)

    act, d_hidden = silu_parts(acc_h[...], acc_d[...])
    act_h[...] = act
    dh_h[...] = d_hidden

    def home_block(block, carry):
        span = columns(block)
        out_h[:, span] = dot(act_h[...], down_w[block]).astype(BF16)
        din_h[:, span] = nt_dot(dh_h[...], up_w[block]).astype(BF16)
        return carry

    lax.fori_loop(0, slots, home_block, 0)

    for copy in d_copies:
        copy.wait_recv()

    acc_hv[...] = dot(vis_tok[:, 0:part], up_w[0])
    acc_dv[...] = nt_dot(vis_scl[:, 0:part], down_w[0])

    def visit_block(block, carry):
        add_up(block, False, vis_tok, acc_hv)
        add_down(block, False, vis_scl, acc_dv)
        return carry

    lax.fori_loop(1, slots, visit_block, 0)
    act, d_hidden = silu_parts(acc_hv[...], acc_dv[...])
    act_v[...] = act
    dh_v[...] = d_hidden

    r_copies = []

    def returns(array):
        for block in range(slots):
            span = pl.ds(block * part, part)
            if array == 0:
                src, dst = ret_out, back_out
                src[:, span] = dot(act_v[...], down_w[block]).astype(BF16)
            else:
                src, dst = ret_din, back_din
                src[:, span] = nt_dot(dh_v[...], up_w[block]).astype(BF16)
            for way, target in enumerate((before, after)):
                lines = pl.ds(way * CAP, CAP)
                copy = remote(
                    src.at[lines, span], dst.at[lines, span], r_s, r_r, (array, block, way),
                    {"expert": target},
                )
                copy.start()
                r_copies.append(copy)
                sends.append(copy)

    hidden_width = act_h.shape[1]

    def up_term(block, dst):
        step = min(256, part)

        def one(i, carry):
            span = pl.ds(pl.multiple_of(block * part + i * step, step), step)
            term = tn_dot(tok[:, span], dh_h[...]) + tn_dot(vis_tok[:, span], dh_v[...])
            dst[pl.ds(pl.multiple_of(i * step, step), step), :] = term.astype(dst.dtype)
            return carry

        lax.fori_loop(0, part // step, one, 0)

    def down_term(block, dst):
        step = 256
        span = columns(block)

        def one(i, carry):
            lines = pl.ds(pl.multiple_of(i * step, step), step)
            term = tn_dot(act_h[:, lines], home_scl[:, span]) + tn_dot(act_v[:, lines], vis_scl[:, span])
            dst[lines, :] = term.astype(dst.dtype)
            return carry

        lax.fori_loop(0, hidden_width // step, one, 0)

    terms = (
        (up_term, up_pair, up_pair_in, up_own, up_x, up_x_in, grad_up),
        (down_term, down_pair, down_pair_in, down_own, down_x, down_x_in, grad_down),
    )
    gp_copies = {}
    gx_copies = {}

    def make_terms(w, k):
        make, pair_out, pair_in, own = terms[w][:4]
        target = lax.rem(high + k, highs) * 2
        make(target + other, pair_out.at[k])
        copy = remote(pair_out.at[k], pair_in.at[k], gp_s, gp_r, (w, k), {"dp": pair})
        copy.start()
        gp_copies[w, k] = copy
        sends.append(copy)
        make(target + low, own.at[k])

    def send_x(w, k):
        pair_in, own, out, into = terms[w][2:6]
        gp_copies[w, k].wait_recv()
        out[k - 1] = (own[k] + pair_in[k].astype(F32)).astype(BF16)
        copy = remote(
            out.at[k - 1], into.at[k - 1], gx_s, gx_r, (w, k - 1),
            {"dp": lax.rem(high + k, highs) * 2 + low},
        )
        copy.start()
        gx_copies[w, k] = copy
        sends.append(copy)

    for k in range(1, highs):
        make_terms(0, k)
    returns(0)
    for k in range(1, highs):
        send_x(0, k)
    for k in range(1, highs):
        make_terms(1, k)
    returns(1)
    for k in range(1, highs):
        send_x(1, k)
    for w in range(2):
        make_terms(w, 0)
    for w in range(2):
        pair_in, own = terms[w][2:4]
        gp_copies[w, 0].wait_recv()
        own[0] = own[0] + pair_in[0].astype(F32)

    for copy in r_copies:
        copy.wait_recv()
    picked = pick[...]
    side = tn_dot(picked, back_out[...])
    mixed[...] = (home_gate * out_h[...].astype(F32) + side_gate * side).astype(BF16)
    side = tn_dot(picked, back_din[...])
    grad_tok[...] = (din_h[...].astype(F32) + side).astype(BF16)

    for w in range(2):
        own, _, into, result = terms[w][3:7]
        whole = own[0]
        for k in range(1, highs):
            gx_copies[w, k].wait_recv()
            whole = whole + into[k - 1].astype(F32)
        result[0] = whole.astype(BF16)
    for copy in sends:
        copy.wait_send()


def local(tokens, cotangent, expert_ids, gate_fix, w_up, w_down):
    rows, width = tokens.shape
    groups = lax.axis_size("groups")
    cycle = lax.axis_size("expert")
    slots = lax.axis_size("dp")
    highs = slots // 2
    hidden = w_up.shape[2]
    part = width // slots
    side = 2 * CAP
    vmem = pl.BlockSpec(memory_space=pltpu.VMEM)
    anywhere = pl.BlockSpec(memory_space=pl.ANY)
    dma = pltpu.SemaphoreType.DMA
    far = highs - 1
    return pl.pallas_call(
        functools.partial(kernel, groups, cycle, slots),
        out_shape=(
            jax.ShapeDtypeStruct((rows, width), BF16),
            jax.ShapeDtypeStruct((rows, width), BF16),
            jax.ShapeDtypeStruct((1, part, hidden), BF16),
            jax.ShapeDtypeStruct((1, hidden, part), BF16),
        ),
        in_specs=[vmem] * 4 + [anywhere] * 2,
        out_specs=[vmem] * 4,
        scratch_shapes=[
            pltpu.VMEM((slots, part, hidden), BF16),
            pltpu.VMEM((slots, hidden, part), BF16),
            pltpu.VMEM((side, rows), BF16),
            pltpu.VMEM((rows, width), BF16),
            pltpu.VMEM((side, width), BF16),
            pltpu.VMEM((side, width), BF16),
            pltpu.VMEM((side, width), BF16),
            pltpu.VMEM((side, width), BF16),
            pltpu.VMEM((rows, hidden), F32),
            pltpu.VMEM((rows, hidden), F32),
            pltpu.VMEM((side, hidden), F32),
            pltpu.VMEM((side, hidden), F32),
            pltpu.VMEM((rows, hidden), BF16),
            pltpu.VMEM((rows, hidden), BF16),
            pltpu.VMEM((side, hidden), BF16),
            pltpu.VMEM((side, hidden), BF16),
            pltpu.VMEM((rows, width), BF16),
            pltpu.VMEM((rows, width), BF16),
            pltpu.VMEM((side, width), BF16),
            pltpu.VMEM((side, width), BF16),
            pltpu.VMEM((side, width), BF16),
            pltpu.VMEM((side, width), BF16),
            pltpu.VMEM((highs, part, hidden), BF16),
            pltpu.VMEM((highs, hidden, part), BF16),
            pltpu.VMEM((highs, part, hidden), BF16),
            pltpu.VMEM((highs, hidden, part), BF16),
            pltpu.VMEM((highs, part, hidden), F32),
            pltpu.VMEM((highs, hidden, part), F32),
            pltpu.VMEM((far, part, hidden), BF16),
            pltpu.VMEM((far, hidden, part), BF16),
            pltpu.VMEM((far, part, hidden), BF16),
            pltpu.VMEM((far, hidden, part), BF16),
            dma((2,)),
            dma((2,)),
            dma((2,)),
            dma((2, far)),
            dma((2, far)),
            dma((2, far, groups - 1)),
            dma((2, far, groups - 1)),
            dma((2, far, groups)),
            dma((2, far, groups)),
            dma((2, 2)),
            dma((2, 2)),
            dma((2, slots, 2)),
            dma((2, slots, 2)),
            dma((2, highs)),
            dma((2, highs)),
            dma((2, far)),
            dma((2, far)),
        ],
        compiler_params=pltpu.CompilerParams(
            collective_id=0, has_side_effects=True, vmem_limit_bytes=56 * 1024 * 1024
        ),
    )(tokens, cotangent, expert_ids, gate_fix, w_up, w_down)


def solution(mesh):
    in_specs = (
        P(("groups", "expert", "dp"), None),
        P(("groups", "expert", "dp"), None),
        P(("groups", "expert", "dp"), None),
        P(("groups", "expert", "dp"), None),
        P("expert", "dp", None),
        P("expert", None, "dp"),
    )
    out_specs = (
        P(("groups", "expert", "dp"), None),
        P(("groups", "expert", "dp"), None),
        P(("groups", "expert"), "dp", None),
        P(("groups", "expert"), None, "dp"),
    )
    return jax.shard_map(local, mesh=mesh, in_specs=in_specs, out_specs=out_specs, check_vma=False)
```

time: 160 us -> 91.2 us (0.57)
  waiting for transfers between devices: 87.3 us -> 0 us
  Pallas kernels: 0 us -> 81.9 us
  matrix products: 24.2 us -> 0 us
  starting transfers between devices: 21.7 us -> 0 us
  between operations: 14.3 us -> 0.66 us
  other arithmetic: 5.83 us -> 0 us
  local copies, waits for them, and re-layouts: 6.11 us -> 8.3 us
    pallas_call x0 -> x1, Pallas kernels: none -> 81.9 us  [local(): pl.pallas_call(functools.partial(kernel, groups, cycle, slots), out_shape...]
    ppermute x8 -> x0, waiting for transfers between devices: 48.2 us -> none  [from_behind(): return lax.ppermute(value, axis, pairs)]
    all_gather x2 -> x0, waiting for transfers between devices: 25.3 us -> none  [the longest x1 25.3 us: local(): lax.all_gather(w_down[0], 'dp', axis=1, tiled=True)]
    dot_general x14 -> x0, matrix products: 24.2 us -> none  [the longest x4 4.05 us: spread_rows(): lax.dot_general(picker, data, (((0,), (0,)), ((), ())), preferred_element...]
    ppermute x8 -> x0, starting transfers between devices: 13.3 us -> none  [from_behind(): return lax.ppermute(value, axis, pairs)]
    all_to_all x2 -> x0, waiting for transfers between devices: 12.4 us -> none  [the longest x1 12.4 us: local(): lax.all_to_all(down_pieces, 'dp', split_axis=0, concat_axis=0, tiled=True)]
    all_to_all x2 -> x0, starting transfers between devices: 8.36 us -> none  [the longest x1 4.67 us: local(): lax.all_to_all(up_pieces, 'dp', split_axis=0, concat_axis=0, tiled=True)]
    reduce_sum x3 -> x0, other arithmetic: 5.01 us -> none  [the longest x1 3.45 us: local(): jnp.sum(got_up.astype(jnp.float32), axis=0).astype(jnp.bfloat16)[None]]
  transfers between devices with their start and end apart: 12 -> 0, of which waited for: 9 -> 0; matrix products, arithmetic and copies ran while one was open for 19% -> 0% of each run, Pallas kernels for 0% -> 0%
where the time goes in v1:
time: 91.2 us; the launch traced here: 90.9 us
  Pallas kernels  81.9 us (90%)
  local copies, waits for them, and re-layouts  8.3 us (9%)
    pallas_call x1, Pallas kernels, local(): pl.pallas_call(functools.partial(kernel, groups, cycle, slots), out_shape...  81.9 us
    unnamed x12, local copies, waits for them, and re-layouts  8.3 us

profile of v1, /device:TPU:0, one launch (start us, length us, event | category | flops | bytes accessed | tf_op | source)
XLA Modules:
  0.0 90.9 jit_solution(10419888863272282643)
XLA Ops:
  0.6 0.0 copy-start.2
  0.6 1.4 %copy.10.ids = s32[128,2]{1,0:T(8,128)} copy(s32[128,2]{0,1:T(2,128)} %param.8) | data formatting | bytes 2048 | tf_op args[2]
  2.1 0.0 copy-done.2
  2.1 0.7 copy.11.fix
  2.8 81.9 %shard_map.93 = (bf16[128,2048]{1,0:T(8,128)(2,1)}, bf16[128,2048]{1,0:T(8,128)(2,1)}, bf16[1,512,768]{2,1,0:T(8,128)(2,1)}, bf16[1,768,512]{2,1,0:T(8,128)(2,1)}) custom-call(bf16[128,2048]{1,0:T(8,128)(2,1)} %tok.1, bf16[128,2048]{1,0:T(8,128)(2,1)} %cot.1, s32[128,2]{1,0:T(8,128)} %copy.10.ids, s32[128,2]{1,0:T(8,128)} %copy.11.fix, ...), custom_call_target="tpu_custom_call" | custom-call | tf_op jit(solution)/shard_map/pallas_call | solution.py:354
  84.7 0.0 copy-start.1
  84.7 2.0 %copy.16 = bf16[128,2048]{1,0:T(8,128)(2,1)} copy(bf16[128,2048]{1,0:T(8,128)(2,1)} %get-tuple-element.8) | data formatting | bytes 1048576
  86.7 1.9 %copy.17 = bf16[128,2048]{1,0:T(8,128)(2,1)} copy(bf16[128,2048]{1,0:T(8,128)(2,1)} %get-tuple-element.9) | data formatting | bytes 1048576
  88.6 0.0 copy-done.1
  88.6 0.0 copy-start
  88.6 0.9 copy.18
  89.4 0.5 copy-done
  90.0 0.9 copy.19
Async XLA Ops:
  0.6 1.4 %copy-start.2 = (s32[128,2]{0,1:T(2,128)S(1)}, s32[128,2]{0,1:T(2,128)}, u32[]{:S(2)}) copy-start(s32[128,2]{0,1:T(2,128)} %param.9) | copy-start | bytes 3076
  84.7 3.8 %copy-start.1 = (bf16[1,512,768]{2,1,0:T(8,128)(2,1)S(1)}, bf16[1,512,768]{2,1,0:T(8,128)(2,1)}, u32[]{:S(2)}) copy-start(bf16[1,512,768]{2,1,0:T(8,128)(2,1)} %get-tuple-element.10) | copy-start | bytes 2359300
  88.6 1.4 %copy-start = (bf16[1,768,512]{2,1,0:T(8,128)(2,1)S(1)}, bf16[1,768,512]{2,1,0:T(8,128)(2,1)}, u32[]{:S(2)}) copy-start(bf16[1,768,512]{2,1,0:T(8,128)(2,1)} %get-tuple-element.11) | copy-start | bytes 2359300

commit v2 on v1

--- a/solution.py
+++ b/solution.py
@@ -46,7 +46,8 @@
 def kernel(
     groups, cycle, slots,
     tok, cot, ids, fix, up_in, down_in,
-    mixed, grad_tok, grad_up, grad_down,
+    mixed_out, grad_tok_out, grad_up_out, grad_down_out,
+    mixed, grad_tok, grad_up, grad_down, out_sem,
     up_w, down_w, pick, home_scl, snd_tok, snd_scl, vis_tok, vis_scl,
     acc_h, acc_d, acc_hv, acc_dv, act_h, dh_h, act_v, dh_v, out_h, din_h,
     ret_out, ret_din, back_out, back_din,
@@ -79,22 +80,27 @@
     for peer in peers:
         pl.semaphore_signal(barrier, inc=1, device_id=peer, device_id_type=MESH)
 
-    goes = jnp.where(ids[:, 1:2] == after, 1.0, 0.0).astype(F32)
     lane = lax.broadcasted_iota(jnp.int32, (rows, rows), 1)
     line = lax.broadcasted_iota(jnp.int32, (rows, rows), 0)
-    flags = jnp.where(lane == 0, goes, 1.0 - goes).astype(BF16)
-    counts = tn_dot(flags, jnp.where(line <= lane, 1.0, 0.0).astype(BF16))
-    marks = tn_dot(flags, jnp.where(line == lane, 1.0, 0.0).astype(BF16))
+    eye = jnp.where(line == lane, 1.0, 0.0).astype(BF16)
+    goes = jnp.where(ids[1:2, :] == after, 1.0, 0.0).astype(F32)
+    upper = lax.broadcasted_iota(jnp.int32, (8, rows), 0) == 0
+    marks = jnp.where(upper, goes, 1.0 - goes)
+    counts = dot(marks.astype(BF16), jnp.where(line <= lane, 1.0, 0.0).astype(BF16))
     slot = lax.broadcasted_iota(jnp.int32, (2 * CAP, rows), 0)
     first = slot < CAP
     wanted = jnp.where(first, slot, slot - CAP).astype(F32) + 1.0
     count = jnp.where(first, counts[0:1, :], counts[1:2, :])
     mark = jnp.where(first, marks[0:1, :], marks[1:2, :])
     pick[...] = jnp.where(count == wanted, mark, 0.0).astype(BF16)
-    fixed = fix[...].astype(F32)
-    total = fixed[:, 0:1] + fixed[:, 1:2]
-    home_gate = fixed[:, 0:1] / total
-    side_gate = fixed[:, 1:2] / total
+    fixed = fix[...]
+    split = jnp.concatenate([fixed // 256, fixed % 256], axis=0).astype(F32).astype(BF16)
+    turned = nt_dot(eye, split)
+    home_fix = turned[:, 0:1] * 256.0 + turned[:, 2:3]
+    side_fix = turned[:, 1:2] * 256.0 + turned[:, 3:4]
+    total = home_fix + side_fix
+    home_gate = home_fix / total
+    side_gate = side_fix / total
 
     pl.semaphore_wait(barrier, len(peers))
 
@@ -326,6 +332,15 @@
     mixed[...] = (home_gate * out_h[...].astype(F32) + side_gate * side).astype(BF16)
     side = tn_dot(picked, back_din[...])
     grad_tok[...] = (din_h[...].astype(F32) + side).astype(BF16)
+    stores = []
+
+    def store(src, dst):
+        copy = pltpu.make_async_copy(src, dst, out_sem.at[len(stores)])
+        copy.start()
+        stores.append(copy)
+
+    store(mixed, mixed_out)
+    store(grad_tok, grad_tok_out)
 
     for w in range(2):
         own, _, into, result = terms[w][3:7]
@@ -334,8 +349,31 @@
             gx_copies[w, k].wait_recv()
             whole = whole + into[k - 1].astype(F32)
         result[0] = whole.astype(BF16)
+        store(result, (grad_up_out, grad_down_out)[w])
+    for copy in stores:
+        copy.wait()
     for copy in sends:
         copy.wait_send()
+
+
+def hand_over(*refs):
+    count = (len(refs) - 1) // 2
+    sems = refs[-1]
+    copies = []
+    for i in range(count):
+        src, dst = refs[i], refs[count + i]
+        middle = src.shape[-2] // 2
+        for j in range(2):
+            span = pl.ds(j * middle, middle)
+            if len(src.shape) == 3:
+                pieces = (src.at[0, span], dst.at[0, span])
+            else:
+                pieces = (src.at[span], dst.at[span])
+            copy = pltpu.make_async_copy(*pieces, sems.at[i, j])
+            copy.start()
+            copies.append(copy)
+    for copy in copies:
+        copy.wait()
 
 
 def local(tokens, cotangent, expert_ids, gate_fix, w_up, w_down):
@@ -351,17 +389,23 @@
     anywhere = pl.BlockSpec(memory_space=pl.ANY)
     dma = pltpu.SemaphoreType.DMA
     far = highs - 1
-    return pl.pallas_call(
+    results = (
+        jax.ShapeDtypeStruct((rows, width), BF16),
+        jax.ShapeDtypeStruct((rows, width), BF16),
+        jax.ShapeDtypeStruct((1, part, hidden), BF16),
+        jax.ShapeDtypeStruct((1, hidden, part), BF16),
+    )
+    made = pl.pallas_call(
         functools.partial(kernel, groups, cycle, slots),
-        out_shape=(
-            jax.ShapeDtypeStruct((rows, width), BF16),
-            jax.ShapeDtypeStruct((rows, width), BF16),
-            jax.ShapeDtypeStruct((1, part, hidden), BF16),
-            jax.ShapeDtypeStruct((1, hidden, part), BF16),
-        ),
+        out_shape=results,
         in_specs=[vmem] * 4 + [anywhere] * 2,
-        out_specs=[vmem] * 4,
+        out_specs=[anywhere] * 4,
         scratch_shapes=[
+            pltpu.VMEM((rows, width), BF16),
+            pltpu.VMEM((rows, width), BF16),
+            pltpu.VMEM((1, part, hidden), BF16),
+            pltpu.VMEM((1, hidden, part), BF16),
+            dma((4,)),
             pltpu.VMEM((slots, part, hidden), BF16),
             pltpu.VMEM((slots, hidden, part), BF16),
             pltpu.VMEM((side, rows), BF16),
@@ -415,7 +459,14 @@
         compiler_params=pltpu.CompilerParams(
             collective_id=0, has_side_effects=True, vmem_limit_bytes=56 * 1024 * 1024
         ),
-    )(tokens, cotangent, expert_ids, gate_fix, w_up, w_down)
+    )(tokens, cotangent, expert_ids.T, gate_fix.T, w_up, w_down)
+    return pl.pallas_call(
+        hand_over,
+        out_shape=results,
+        in_specs=[anywhere] * 4,
+        out_specs=[anywhere] * 4,
+        scratch_shapes=[dma((4, 2))],
+    )(*made)
 
 
 def solution(mesh):

time: 91.2 us -> 163 us (1.79)
  Pallas kernels: 81.9 us -> 162 us
  local copies, waits for them, and re-layouts: 8.3 us -> 0 us
    pallas_call x0 -> x1, Pallas kernels: none -> 80.6 us  [local(): pl.pallas_call(hand_over, out_shape=results, in_specs=[anywhere] * 4, out...]
    unnamed x12 -> x0, local copies, waits for them, and re-layouts: 8.3 us -> none
where the time goes in v2:
time: 163 us
  Pallas kernels  162 us (99%)
    pallas_call x1, Pallas kernels, local(): pl.pallas_call(functools.partial(kernel, groups, cycle, slots), out_shape...  81.4 us
    pallas_call x1, Pallas kernels, local(): pl.pallas_call(hand_over, out_shape=results, in_specs=[anywhere] * 4, out...  80.6 us

profile of v2, /device:TPU:0, one launch (start us, length us, event | category | flops | bytes accessed | tf_op | source)
XLA Modules:
  0.0 162.6 jit_solution(6782175423634252270)
XLA Ops:
  0.6 81.4 %shard_map.93 = (bf16[128,2048]{1,0:T(8,128)(2,1)}, bf16[128,2048]{1,0:T(8,128)(2,1)}, bf16[1,512,768]{2,1,0:T(8,128)(2,1)}, bf16[1,768,512]{2,1,0:T(8,128)(2,1)}) custom-call(bf16[128,2048]{1,0:T(8,128)(2,1)} %tok.1, bf16[128,2048]{1,0:T(8,128)(2,1)} %cot.1, s32[2,128]{1,0:T(2,128)} %bitcast.2, s32[2,128]{1,0:T(2,128)} %bitcast.3, ...), custom_call_target="tpu_custom_call" | custom-call | tf_op jit(solution)/shard_map/pallas_call | solution.py:398
  82.0 80.6 %shard_map.94 = (bf16[128,2048]{1,0:T(8,128)(2,1)}, bf16[128,2048]{1,0:T(8,128)(2,1)}, bf16[1,512,768]{2,1,0:T(8,128)(2,1)}, bf16[1,768,512]{2,1,0:T(8,128)(2,1)}) custom-call(bf16[128,2048]{1,0:T(8,128)(2,1)} %get-tuple-element.8.refs_0_, bf16[128,2048]{1,0:T(8,128)(2,1)} %get-tuple-element.9.refs_1_, bf16[1,512,768]{2,1,0:T(8,128)(2,1)} %get-tuple-element.10.refs_2_, ...), custom_call_target="tpu_custom_call" | custom-call | tf_op jit(solution)/shard_map/pallas_call | solution.py:463

commit v3 on v2

--- a/solution.py
+++ b/solution.py
@@ -34,13 +34,6 @@
         device_id=device,
         device_id_type=MESH,
     )
-
-
-def silu_parts(hidden, d_act):
-    sig = 1.0 / (1.0 + jnp.exp(-hidden))
-    act = (hidden * sig).astype(BF16)
-    d_hidden = (d_act * sig * (1.0 + hidden * (1.0 - sig))).astype(BF16)
-    return act, d_hidden
 
 
 def kernel(
@@ -102,11 +95,30 @@
     home_gate = home_fix / total
     side_gate = side_fix / total
 
+    sends = []
+
+    def begin(copy):
+        copy.start()
+        sends.append(copy)
+        return copy
+
+    ways = ((0, after), (1, before))
+    order = [(k, h) for k in list(range(1, highs)) + [0] for h in (other, low)]
+    order = [lax.rem(high + k, highs) * 2 + h for k, h in order]
+    far = 2 * (highs - 1)
+
+    picked = pick[...]
+    snd_tok[...] = dot(picked, tok[...]).astype(BF16)
     pl.semaphore_wait(barrier, len(peers))
+
+    tok_copies = []
+    for way, target in ways:
+        span = pl.ds(way * CAP, CAP)
+        copy = remote(snd_tok.at[span], vis_tok.at[span], d_s, d_r, (slots, way), {"expert": target})
+        tok_copies.append(begin(copy))
 
     weights = ((up_in, up_w), (down_in, down_w))
     local_copies = []
-    sends = []
     pair_copies = []
     x_copies = [[], []]
     for w, (own, full) in enumerate(weights):
@@ -117,33 +129,24 @@
                 own.at[0, mine], full.at[me, mine], x_s, x_r, (w, k - 1),
                 {"dp": lax.rem(high + k, highs) * 2 + low},
             )
-            copy.start()
-            x_copies[w].append(copy)
-            sends.append(copy)
+            x_copies[w].append(begin(copy))
         copy = remote(own.at[0], full.at[me], pair_s, pair_r, w, {"dp": pair})
-        copy.start()
-        pair_copies.append(copy)
-        sends.append(copy)
+        pair_copies.append(begin(copy))
         copy = pltpu.make_async_copy(own.at[0], full.at[me], local_sem.at[w])
         copy.start()
         local_copies.append(copy)
 
-    picked = pick[...]
-    d_copies = []
-
-    def dispatch(array, src, dst):
-        for way, target in enumerate((after, before)):
-            span = pl.ds(way * CAP, CAP)
-            copy = remote(src.at[span], dst.at[span], d_s, d_r, (array, way), {"expert": target})
-            copy.start()
-            d_copies.append(copy)
-            sends.append(copy)
-
-    snd_tok[...] = dot(picked, tok[...]).astype(BF16)
-    dispatch(0, snd_tok, vis_tok)
     wide = cot[...].astype(F32)
     snd_scl[...] = dot(picked, (side_gate * wide).astype(BF16)).astype(BF16)
-    dispatch(1, snd_scl, vis_scl)
+    scl_copies = []
+    for r, block in enumerate(order):
+        for way, target in ways:
+            lines = pl.ds(way * CAP, CAP)
+            copy = remote(
+                snd_scl.at[lines, columns(block)], vis_scl.at[lines, columns(block)], d_s, d_r, (r, way),
+                {"expert": target},
+            )
+            scl_copies.append(begin(copy))
     home_scl[...] = (home_gate * wide).astype(BF16)
 
     def add_up(block, first_one, src, acc):
@@ -154,60 +157,69 @@
         term = nt_dot(src[:, columns(block)], down_w[block])
         acc[...] = term if first_one else acc[...] + term
 
-    adders = ((add_up, tok, acc_h), (add_down, home_scl, acc_d))
-
-    for w, (add, src, acc) in enumerate(adders):
-        local_copies[w].wait()
-        add(me, True, src, acc)
-    for w, (add, src, acc) in enumerate(adders):
-        pair_copies[w].wait_recv()
-        add(pair, False, src, acc)
+    def forward_x(w, k):
+        own, full = weights[w]
+        came = lax.rem(high + highs - k, highs) * 2 + low
+        half = own.shape[1] // groups
+        x_copies[w][k - 1].wait_recv()
+        piece = full.at[came, pl.ds(pl.multiple_of(group * half, half), half)]
+        for q in range(1, groups):
+            y_copies[w, k, q] = begin(remote(
+                piece, piece, y_s, y_r, (w, k - 1, q - 1), {"groups": lax.rem(group + q, groups)}
+            ))
+        f_copies[w, k, 0] = begin(remote(piece, piece, f_s, f_r, (w, k - 1, 0), {"dp": pair}))
+
+    def forward_y(w, k):
+        own, full = weights[w]
+        came = lax.rem(high + highs - k, highs) * 2 + low
+        half = own.shape[1] // groups
+        for q in range(1, groups):
+            y_copies[w, k, q].wait_recv()
+            theirs = lax.rem(group + groups - q, groups)
+            piece = full.at[came, pl.ds(pl.multiple_of(theirs * half, half), half)]
+            f_copies[w, k, q] = begin(remote(piece, piece, f_s, f_r, (w, k - 1, q), {"dp": pair}))
 
     y_copies = {}
     f_copies = {}
-    for k in range(1, highs):
+    local_copies[0].wait()
+    add_up(me, True, tok, acc_h)
+    pair_copies[0].wait_recv()
+    add_up(pair, False, tok, acc_h)
+    local_copies[1].wait()
+    add_down(me, True, home_scl, acc_d)
+    for k in range(1, highs):
+        forward_x(0, k)
+    pair_copies[1].wait_recv()
+    add_down(pair, False, home_scl, acc_d)
+    for copy in tok_copies:
+        copy.wait_recv()
+    add_up(me, True, vis_tok, acc_hv)
+    add_up(pair, False, vis_tok, acc_hv)
+    for k in range(1, highs):
+        forward_x(1, k)
+    for k in range(1, highs):
+        forward_y(0, k)
         came = lax.rem(high + highs - k, highs) * 2 + low
-        for w, (own, full) in enumerate(weights):
-            half = own.shape[1] // groups
-            mine = pl.ds(pl.multiple_of(group * half, half), half)
-            x_copies[w][k - 1].wait_recv()
-            piece = full.at[came, mine]
-            for q in range(1, groups):
-                copy = remote(
-                    piece, piece, y_s, y_r, (w, k - 1, q - 1), {"groups": lax.rem(group + q, groups)}
-                )
-                copy.start()
-                y_copies[w, k, q] = copy
-                sends.append(copy)
-            copy = remote(piece, piece, f_s, f_r, (w, k - 1, 0), {"dp": pair})
-            copy.start()
-            f_copies[w, k, 0] = copy
-            sends.append(copy)
-    for k in range(1, highs):
-        came = lax.rem(high + highs - k, highs) * 2 + low
-        for w, (own, full) in enumerate(weights):
-            half = own.shape[1] // groups
-            for q in range(1, groups):
-                y_copies[w, k, q].wait_recv()
-                theirs = lax.rem(group + groups - q, groups)
-                piece = full.at[came, pl.ds(pl.multiple_of(theirs * half, half), half)]
-                copy = remote(piece, piece, f_s, f_r, (w, k - 1, q), {"dp": pair})
-                copy.start()
-                f_copies[w, k, q] = copy
-                sends.append(copy)
-            add, src, acc = adders[w]
-            add(came, False, src, acc)
-    for k in range(1, highs):
+        add_up(came, False, tok, acc_h)
+        add_up(came, False, vis_tok, acc_hv)
+    for k in range(1, highs):
+        for q in range(groups):
+            f_copies[0, k, q].wait_recv()
         came = lax.rem(high + highs - k, highs) * 2 + other
-        for w in range(2):
-            for q in range(groups):
-                f_copies[w, k, q].wait_recv()
-            add, src, acc = adders[w]
-            add(came, False, src, acc)
-
-    act, d_hidden = silu_parts(acc_h[...], acc_d[...])
-    act_h[...] = act
-    dh_h[...] = d_hidden
+        add_up(came, False, tok, acc_h)
+        add_up(came, False, vis_tok, acc_hv)
+
+    def activate(acc, act):
+        hidden = acc[...]
+        act[...] = (hidden * (1.0 / (1.0 + jnp.exp(-hidden)))).astype(BF16)
+
+    def back_through(acc, d_acc, out):
+        hidden = acc[...]
+        sig = 1.0 / (1.0 + jnp.exp(-hidden))
+        out[...] = (d_acc[...] * sig * (1.0 + hidden * (1.0 - sig))).astype(BF16)
+
+    activate(acc_h, act_h)
+    activate(acc_hv, act_v)
 
     def home_block(block, carry):
         span = columns(block)
@@ -215,25 +227,7 @@
         din_h[:, span] = nt_dot(dh_h[...], up_w[block]).astype(BF16)
         return carry
 
-    lax.fori_loop(0, slots, home_block, 0)
-
-    for copy in d_copies:
-        copy.wait_recv()
-
-    acc_hv[...] = dot(vis_tok[:, 0:part], up_w[0])
-    acc_dv[...] = nt_dot(vis_scl[:, 0:part], down_w[0])
-
-    def visit_block(block, carry):
-        add_up(block, False, vis_tok, acc_hv)
-        add_down(block, False, vis_scl, acc_dv)
-        return carry
-
-    lax.fori_loop(1, slots, visit_block, 0)
-    act, d_hidden = silu_parts(acc_hv[...], acc_dv[...])
-    act_v[...] = act
-    dh_v[...] = d_hidden
-
-    r_copies = []
+    r_copies = [[], []]
 
     def returns(array):
         for block in range(slots):
@@ -246,13 +240,10 @@
                 src[:, span] = nt_dot(dh_v[...], up_w[block]).astype(BF16)
             for way, target in enumerate((before, after)):
                 lines = pl.ds(way * CAP, CAP)
-                copy = remote(
+                r_copies[array].append(begin(remote(
                     src.at[lines, span], dst.at[lines, span], r_s, r_r, (array, block, way),
                     {"expert": target},
-                )
-                copy.start()
-                r_copies.append(copy)
-                sends.append(copy)
+                )))
 
     hidden_width = act_h.shape[1]
 
@@ -308,30 +299,42 @@
         gx_copies[w, k] = copy
         sends.append(copy)
 
+    for copy in scl_copies[: 2 * far]:
+        copy.wait_recv()
+    for k in range(1, highs):
+        make_terms(1, k)
+    for k in range(1, highs):
+        forward_y(1, k)
+    for k in range(1, highs):
+        send_x(1, k)
+    for k in range(1, highs):
+        add_down(lax.rem(high + highs - k, highs) * 2 + low, False, home_scl, acc_d)
+    for k in range(1, highs):
+        for q in range(groups):
+            f_copies[1, k, q].wait_recv()
+        add_down(lax.rem(high + highs - k, highs) * 2 + other, False, home_scl, acc_d)
+    returns(0)
+    back_through(acc_h, acc_d, dh_h)
+    for r, block in enumerate(order[:far]):
+        add_down(block, r == 0, vis_scl, acc_dv)
+    for copy in scl_copies[2 * far :]:
+        copy.wait_recv()
+    for block in order[far:]:
+        add_down(block, False, vis_scl, acc_dv)
+    back_through(acc_hv, acc_dv, dh_v)
     for k in range(1, highs):
         make_terms(0, k)
-    returns(0)
+    returns(1)
     for k in range(1, highs):
         send_x(0, k)
-    for k in range(1, highs):
-        make_terms(1, k)
-    returns(1)
-    for k in range(1, highs):
-        send_x(1, k)
-    for w in range(2):
+    for w in (1, 0):
         make_terms(w, 0)
-    for w in range(2):
+    lax.fori_loop(0, slots, home_block, 0)
+    for w in (1, 0):
         pair_in, own = terms[w][2:4]
         gp_copies[w, 0].wait_recv()
         own[0] = own[0] + pair_in[0].astype(F32)
 
-    for copy in r_copies:
-        copy.wait_recv()
-    picked = pick[...]
-    side = tn_dot(picked, back_out[...])
-    mixed[...] = (home_gate * out_h[...].astype(F32) + side_gate * side).astype(BF16)
-    side = tn_dot(picked, back_din[...])
-    grad_tok[...] = (din_h[...].astype(F32) + side).astype(BF16)
     stores = []
 
     def store(src, dst):
@@ -339,10 +342,7 @@
         copy.start()
         stores.append(copy)
 
-    store(mixed, mixed_out)
-    store(grad_tok, grad_tok_out)
-
-    for w in range(2):
+    def finish(w):
         own, _, into, result = terms[w][3:7]
         whole = own[0]
         for k in range(1, highs):
@@ -350,6 +350,20 @@
             whole = whole + into[k - 1].astype(F32)
         result[0] = whole.astype(BF16)
         store(result, (grad_up_out, grad_down_out)[w])
+
+    picked = pick[...]
+    for copy in r_copies[0]:
+        copy.wait_recv()
+    side = tn_dot(picked, back_out[...])
+    mixed[...] = (home_gate * out_h[...].astype(F32) + side_gate * side).astype(BF16)
+    store(mixed, mixed_out)
+    finish(1)
+    for copy in r_copies[1]:
+        copy.wait_recv()
+    side = tn_dot(picked, back_din[...])
+    grad_tok[...] = (din_h[...].astype(F32) + side).astype(BF16)
+    store(grad_tok, grad_tok_out)
+    finish(0)
     for copy in stores:
         copy.wait()
     for copy in sends:
@@ -357,22 +371,29 @@
 
 
 def hand_over(*refs):
-    count = (len(refs) - 1) // 2
-    sems = refs[-1]
-    copies = []
+    count = (len(refs) - 2) // 3
+    sems, done = refs[-2:]
+    loads, stores = [], []
+
+    def piece(ref, j):
+        middle = ref.shape[-2] // 2
+        span = pl.ds(j * middle, middle)
+        return ref.at[0, span] if len(ref.shape) == 3 else ref.at[span]
+
     for i in range(count):
-        src, dst = refs[i], refs[count + i]
-        middle = src.shape[-2] // 2
         for j in range(2):
-            span = pl.ds(j * middle, middle)
-            if len(src.shape) == 3:
-                pieces = (src.at[0, span], dst.at[0, span])
-            else:
-                pieces = (src.at[span], dst.at[span])
-            copy = pltpu.make_async_copy(*pieces, sems.at[i, j])
+            copy = pltpu.make_async_copy(piece(refs[i], j), piece(refs[2 * count + i], j), sems.at[i, j])
             copy.start()
-            copies.append(copy)
-    for copy in copies:
+            loads.append(copy)
+    for i in range(count):
+        for j in range(2):
+            loads[2 * i + j].wait()
+            copy = pltpu.make_async_copy(
+                piece(refs[2 * count + i], j), piece(refs[count + i], j), done.at[i, j]
+            )
+            copy.start()
+            stores.append(copy)
+    for copy in stores:
         copy.wait()
 
 
@@ -447,8 +468,8 @@
             dma((2, far, groups - 1)),
             dma((2, far, groups)),
             dma((2, far, groups)),
-            dma((2, 2)),
-            dma((2, 2)),
+            dma((slots + 1, 2)),
+            dma((slots + 1, 2)),
             dma((2, slots, 2)),
             dma((2, slots, 2)),
             dma((2, highs)),
@@ -465,7 +486,7 @@
         out_shape=results,
         in_specs=[anywhere] * 4,
         out_specs=[anywhere] * 4,
-        scratch_shapes=[dma((4, 2))],
+        scratch_shapes=[pltpu.VMEM(shape.shape, BF16) for shape in results] + [dma((4, 2)), dma((4, 2))],
     )(*made)
 
 

time: 163 us -> 74 us (0.45)
  Pallas kernels: 162 us -> 73.2 us
    pallas_call x1, Pallas kernels: 80.6 us -> 2.59 us  [local(): pl.pallas_call(hand_over, out_shape=results, in_specs=[anywhere] * 4, out...]
    pallas_call x1, Pallas kernels: 81.4 us -> 70.6 us  [local(): pl.pallas_call(functools.partial(kernel, groups, cycle, slots), out_shape...]
where the time goes in v3:
time: 74 us; the launch traced here: 73.8 us
  Pallas kernels  73.2 us (99%)
    pallas_call x1, Pallas kernels, local(): pl.pallas_call(functools.partial(kernel, groups, cycle, slots), out_shape...  70.6 us
    pallas_call x1, Pallas kernels, local(): pl.pallas_call(hand_over, out_shape=results, in_specs=[anywhere] * 4, out...  2.59 us

profile of v3, /device:TPU:0, one launch (start us, length us, event | category | flops | bytes accessed | tf_op | source)
XLA Modules:
  0.0 73.8 jit_solution(5143951582367494885)
XLA Ops:
  0.6 70.6 %shard_map.93 = (bf16[128,2048]{1,0:T(8,128)(2,1)}, bf16[128,2048]{1,0:T(8,128)(2,1)}, bf16[1,512,768]{2,1,0:T(8,128)(2,1)}, bf16[1,768,512]{2,1,0:T(8,128)(2,1)}) custom-call(bf16[128,2048]{1,0:T(8,128)(2,1)} %tok.1, bf16[128,2048]{1,0:T(8,128)(2,1)} %cot.1, s32[2,128]{1,0:T(2,128)} %bitcast.2, s32[2,128]{1,0:T(2,128)} %bitcast.3, ...), custom_call_target="tpu_custom_call" | custom-call | tf_op jit(solution)/shard_map/pallas_call | solution.py:419
  71.2 2.6 %shard_map.94 = (bf16[128,2048]{1,0:T(8,128)(2,1)}, bf16[128,2048]{1,0:T(8,128)(2,1)}, bf16[1,512,768]{2,1,0:T(8,128)(2,1)}, bf16[1,768,512]{2,1,0:T(8,128)(2,1)}) custom-call(bf16[128,2048]{1,0:T(8,128)(2,1)} %get-tuple-element.8.refs_0_, bf16[128,2048]{1,0:T(8,128)(2,1)} %get-tuple-element.9.refs_1_, bf16[1,512,768]{2,1,0:T(8,128)(2,1)} %get-tuple-element.10.refs_2_, ...), custom_call_target="tpu_custom_call" | custom-call | tf_op jit(solution)/shard_map/pallas_call | solution.py:484

commit v4 on v3

--- a/solution.py
+++ b/solution.py
@@ -8,6 +8,7 @@
 from jax.sharding import PartitionSpec as P
 
 CAP = 80
+HALVES = 2
 MESH = pl.DeviceIdType.MESH
 F32 = jnp.float32
 BF16 = jnp.bfloat16
@@ -106,6 +107,9 @@
     order = [(k, h) for k in list(range(1, highs)) + [0] for h in (other, low)]
     order = [lax.rem(high + k, highs) * 2 + h for k, h in order]
     far = 2 * (highs - 1)
+    part_half = part // HALVES
+    pieces = [(block, m) for m in range(HALVES) for block in order[:far]]
+    pieces += [(block, m) for m in range(HALVES) for block in order[far:]]
 
     picked = pick[...]
     snd_tok[...] = dot(picked, tok[...]).astype(BF16)
@@ -114,7 +118,7 @@
     tok_copies = []
     for way, target in ways:
         span = pl.ds(way * CAP, CAP)
-        copy = remote(snd_tok.at[span], vis_tok.at[span], d_s, d_r, (slots, way), {"expert": target})
+        copy = remote(snd_tok.at[span], vis_tok.at[span], d_s, d_r, (slots * HALVES, way), {"expert": target})
         tok_copies.append(begin(copy))
 
     weights = ((up_in, up_w), (down_in, down_w))
@@ -139,12 +143,12 @@
     wide = cot[...].astype(F32)
     snd_scl[...] = dot(picked, (side_gate * wide).astype(BF16)).astype(BF16)
     scl_copies = []
-    for r, block in enumerate(order):
+    for r, (block, m) in enumerate(pieces):
+        span = pl.ds(pl.multiple_of(block * part + m * part_half, part_half), part_half)
         for way, target in ways:
             lines = pl.ds(way * CAP, CAP)
             copy = remote(
-                snd_scl.at[lines, columns(block)], vis_scl.at[lines, columns(block)], d_s, d_r, (r, way),
-                {"expert": target},
+                snd_scl.at[lines, span], vis_scl.at[lines, span], d_s, d_r, (r, way), {"expert": target}
             )
             scl_copies.append(begin(copy))
     home_scl[...] = (home_gate * wide).astype(BF16)
@@ -247,28 +251,34 @@
 
     hidden_width = act_h.shape[1]
 
-    def up_term(block, dst):
-        step = min(256, part)
+    def up_term(block, m, dst):
+        step = min(256, part_half)
 
         def one(i, carry):
-            span = pl.ds(pl.multiple_of(block * part + i * step, step), step)
+            start = m * part_half + i * step
+            span = pl.ds(pl.multiple_of(block * part + start, step), step)
             term = tn_dot(tok[:, span], dh_h[...]) + tn_dot(vis_tok[:, span], dh_v[...])
-            dst[pl.ds(pl.multiple_of(i * step, step), step), :] = term.astype(dst.dtype)
+            dst[pl.ds(pl.multiple_of(start, step), step), :] = term.astype(dst.dtype)
             return carry
 
-        lax.fori_loop(0, part // step, one, 0)
-
-    def down_term(block, dst):
+        lax.fori_loop(0, part_half // step, one, 0)
+
+    def down_term(block, m, dst):
         step = 256
-        span = columns(block)
+        span = pl.ds(pl.multiple_of(block * part + m * part_half, part_half), part_half)
+        into = pl.ds(m * part_half, part_half)
 
         def one(i, carry):
             lines = pl.ds(pl.multiple_of(i * step, step), step)
             term = tn_dot(act_h[:, lines], home_scl[:, span]) + tn_dot(act_v[:, lines], vis_scl[:, span])
-            dst[lines, :] = term.astype(dst.dtype)
+            dst[lines, into] = term.astype(dst.dtype)
             return carry
 
         lax.fori_loop(0, hidden_width // step, one, 0)
+
+    def cut(w, k, m):
+        span = pl.ds(m * part_half, part_half)
+        return (k, span) if w == 0 else (k, slice(None), span)
 
     terms = (
         (up_term, up_pair, up_pair_in, up_own, up_x, up_x_in, grad_up),
@@ -277,36 +287,36 @@
     gp_copies = {}
     gx_copies = {}
 
-    def make_terms(w, k):
+    def make_terms(w, k, m):
         make, pair_out, pair_in, own = terms[w][:4]
         target = lax.rem(high + k, highs) * 2
-        make(target + other, pair_out.at[k])
-        copy = remote(pair_out.at[k], pair_in.at[k], gp_s, gp_r, (w, k), {"dp": pair})
-        copy.start()
-        gp_copies[w, k] = copy
-        sends.append(copy)
-        make(target + low, own.at[k])
-
-    def send_x(w, k):
+        make(target + other, m, pair_out.at[k])
+        where = cut(w, k, m)
+        gp_copies[w, k, m] = begin(remote(
+            pair_out.at[where], pair_in.at[where], gp_s, gp_r, (w, k, m), {"dp": pair}
+        ))
+        make(target + low, m, own.at[k])
+
+    def send_x(w, k, m):
         pair_in, own, out, into = terms[w][2:6]
-        gp_copies[w, k].wait_recv()
-        out[k - 1] = (own[k] + pair_in[k].astype(F32)).astype(BF16)
-        copy = remote(
-            out.at[k - 1], into.at[k - 1], gx_s, gx_r, (w, k - 1),
+        gp_copies[w, k, m].wait_recv()
+        where = cut(w, k, m)
+        there = cut(w, k - 1, m)
+        out[there] = (own[where] + pair_in[where].astype(F32)).astype(BF16)
+        gx_copies[w, k, m] = begin(remote(
+            out.at[there], into.at[there], gx_s, gx_r, (w, k - 1, m),
             {"dp": lax.rem(high + k, highs) * 2 + low},
-        )
-        copy.start()
-        gx_copies[w, k] = copy
-        sends.append(copy)
-
-    for copy in scl_copies[: 2 * far]:
-        copy.wait_recv()
-    for k in range(1, highs):
-        make_terms(1, k)
+        ))
+
+    for m in range(HALVES):
+        for copy in scl_copies[2 * far * m : 2 * far * (m + 1)]:
+            copy.wait_recv()
+        for k in range(1, highs):
+            make_terms(1, k, m)
+        for k in range(1, highs):
+            send_x(1, k, m)
     for k in range(1, highs):
         forward_y(1, k)
-    for k in range(1, highs):
-        send_x(1, k)
     for k in range(1, highs):
         add_down(lax.rem(high + highs - k, highs) * 2 + low, False, home_scl, acc_d)
     for k in range(1, highs):
@@ -317,22 +327,25 @@
     back_through(acc_h, acc_d, dh_h)
     for r, block in enumerate(order[:far]):
         add_down(block, r == 0, vis_scl, acc_dv)
-    for copy in scl_copies[2 * far :]:
+    for copy in scl_copies[2 * far * HALVES :]:
         copy.wait_recv()
     for block in order[far:]:
         add_down(block, False, vis_scl, acc_dv)
     back_through(acc_hv, acc_dv, dh_v)
-    for k in range(1, highs):
-        make_terms(0, k)
+    for m in range(HALVES):
+        for k in range(1, highs):
+            make_terms(0, k, m)
+        for k in range(1, highs):
+            send_x(0, k, m)
     returns(1)
-    for k in range(1, highs):
-        send_x(0, k)
     for w in (1, 0):
-        make_terms(w, 0)
+        for m in range(HALVES):
+            make_terms(w, 0, m)
     lax.fori_loop(0, slots, home_block, 0)
     for w in (1, 0):
         pair_in, own = terms[w][2:4]
-        gp_copies[w, 0].wait_recv()
+        for m in range(HALVES):
+            gp_copies[w, 0, m].wait_recv()
         own[0] = own[0] + pair_in[0].astype(F32)
 
     stores = []
@@ -342,28 +355,41 @@
         copy.start()
         stores.append(copy)
 
-    def finish(w):
+    def finish(w, m):
         own, _, into, result = terms[w][3:7]
-        whole = own[0]
+        where = cut(w, 0, m)
+        whole = own[where]
         for k in range(1, highs):
-            gx_copies[w, k].wait_recv()
-            whole = whole + into[k - 1].astype(F32)
-        result[0] = whole.astype(BF16)
-        store(result, (grad_up_out, grad_down_out)[w])
+            gx_copies[w, k, m].wait_recv()
+            whole = whole + into[cut(w, k - 1, m)].astype(F32)
+        result[where] = whole.astype(BF16)
+        store(result.at[where], (grad_up_out, grad_down_out)[w].at[where])
 
     picked = pick[...]
-    for copy in r_copies[0]:
-        copy.wait_recv()
-    side = tn_dot(picked, back_out[...])
-    mixed[...] = (home_gate * out_h[...].astype(F32) + side_gate * side).astype(BF16)
+
+    def combine(array, block):
+        for copy in r_copies[array][2 * block : 2 * block + 2]:
+            copy.wait_recv()
+        span = pl.ds(block * part, part)
+        if array == 0:
+            side = tn_dot(picked, back_out[:, span])
+            value = home_gate * out_h[:, span].astype(F32) + side_gate * side
+            mixed[:, span] = value.astype(BF16)
+        else:
+            side = tn_dot(picked, back_din[:, span])
+            grad_tok[:, span] = (din_h[:, span].astype(F32) + side).astype(BF16)
+
+    for block in range(slots):
+        combine(0, block)
     store(mixed, mixed_out)
-    finish(1)
-    for copy in r_copies[1]:
-        copy.wait_recv()
-    side = tn_dot(picked, back_din[...])
-    grad_tok[...] = (din_h[...].astype(F32) + side).astype(BF16)
+    for m in range(HALVES):
+        finish(1, m)
+    for m in range(HALVES - 1):
+        finish(0, m)
+    for block in range(slots):
+        combine(1, block)
     store(grad_tok, grad_tok_out)
-    finish(0)
+    finish(0, HALVES - 1)
     for copy in stores:
         copy.wait()
     for copy in sends:
@@ -426,7 +452,7 @@
             pltpu.VMEM((rows, width), BF16),
             pltpu.VMEM((1, part, hidden), BF16),
             pltpu.VMEM((1, hidden, part), BF16),
-            dma((4,)),
+            dma((2 + 2 * HALVES,)),
             pltpu.VMEM((slots, part, hidden), BF16),
             pltpu.VMEM((slots, hidden, part), BF16),
             pltpu.VMEM((side, rows), BF16),
@@ -468,14 +494,14 @@
             dma((2, far, groups - 1)),
             dma((2, far, groups)),
             dma((2, far, groups)),
-            dma((slots + 1, 2)),
-            dma((slots + 1, 2)),
+            dma((slots * HALVES + 1, 2)),
+            dma((slots * HALVES + 1, 2)),
             dma((2, slots, 2)),
             dma((2, slots, 2)),
-            dma((2, highs)),
-            dma((2, highs)),
-            dma((2, far)),
-            dma((2, far)),
+            dma((2, highs, HALVES)),
+            dma((2, highs, HALVES)),
+            dma((2, far, HALVES)),
+            dma((2, far, HALVES)),
         ],
         compiler_params=pltpu.CompilerParams(
             collective_id=0, has_side_effects=True, vmem_limit_bytes=56 * 1024 * 1024

time: 74 us -> 72.1 us (0.974)
  Pallas kernels: 73.2 us -> 71.2 us
    pallas_call x1, Pallas kernels: 70.6 us -> 68.6 us  [local(): pl.pallas_call(functools.partial(kernel, groups, cycle, slots), out_shape...]
where the time goes in v4:
time: 72.1 us; the launch traced here: 71.8 us
  Pallas kernels  71.2 us (99%)
    pallas_call x1, Pallas kernels, local(): pl.pallas_call(functools.partial(kernel, groups, cycle, slots), out_shape...  68.6 us
    pallas_call x1, Pallas kernels, local(): pl.pallas_call(hand_over, out_shape=results, in_specs=[anywhere] * 4, out...  2.59 us

profile of v4, /device:TPU:0, one launch (start us, length us, event | category | flops | bytes accessed | tf_op | source)
XLA Modules:
  0.0 71.8 jit_solution(4305966638307458713)
XLA Ops:
  0.6 68.6 %shard_map.93 = (bf16[128,2048]{1,0:T(8,128)(2,1)}, bf16[128,2048]{1,0:T(8,128)(2,1)}, bf16[1,512,768]{2,1,0:T(8,128)(2,1)}, bf16[1,768,512]{2,1,0:T(8,128)(2,1)}) custom-call(bf16[128,2048]{1,0:T(8,128)(2,1)} %tok.1, bf16[128,2048]{1,0:T(8,128)(2,1)} %cot.1, s32[2,128]{1,0:T(2,128)} %bitcast.2, s32[2,128]{1,0:T(2,128)} %bitcast.3, ...), custom_call_target="tpu_custom_call" | custom-call | tf_op jit(solution)/shard_map/pallas_call | solution.py:445
  69.2 2.6 %shard_map.94 = (bf16[128,2048]{1,0:T(8,128)(2,1)}, bf16[128,2048]{1,0:T(8,128)(2,1)}, bf16[1,512,768]{2,1,0:T(8,128)(2,1)}, bf16[1,768,512]{2,1,0:T(8,128)(2,1)}) custom-call(bf16[128,2048]{1,0:T(8,128)(2,1)} %get-tuple-element.8.refs_0_, bf16[128,2048]{1,0:T(8,128)(2,1)} %get-tuple-element.9.refs_1_, bf16[1,512,768]{2,1,0:T(8,128)(2,1)} %get-tuple-element.10.refs_2_, ...), custom_call_target="tpu_custom_call" | custom-call | tf_op jit(solution)/shard_map/pallas_call | solution.py:510

commit v5 on v4

--- a/solution.py
+++ b/solution.py
@@ -318,12 +318,12 @@
     for k in range(1, highs):
         forward_y(1, k)
     for k in range(1, highs):
-        add_down(lax.rem(high + highs - k, highs) * 2 + low, False, home_scl, acc_d)
-    for k in range(1, highs):
         for q in range(groups):
             f_copies[1, k, q].wait_recv()
+    returns(0)
+    for k in range(1, highs):
+        add_down(lax.rem(high + highs - k, highs) * 2 + low, False, home_scl, acc_d)
         add_down(lax.rem(high + highs - k, highs) * 2 + other, False, home_scl, acc_d)
-    returns(0)
     back_through(acc_h, acc_d, dh_h)
     for r, block in enumerate(order[:far]):
         add_down(block, r == 0, vis_scl, acc_dv)

time: 72.1 us -> 71.6 us (level)
  no operation moved by 1% of the time
where the time goes in v5:
time: 71.6 us; the launch traced here: 71.2 us
  Pallas kernels  70.6 us (99%)
    pallas_call x1, Pallas kernels, local(): pl.pallas_call(functools.partial(kernel, groups, cycle, slots), out_shape...  68 us
    pallas_call x1, Pallas kernels, local(): pl.pallas_call(hand_over, out_shape=results, in_specs=[anywhere] * 4, out...  2.59 us

profile of v5, /device:TPU:0, one launch (start us, length us, event | category | flops | bytes accessed | tf_op | source)
XLA Modules:
  0.0 71.2 jit_solution(1050310840564957748)
XLA Ops:
  0.6 68.0 %shard_map.93 = (bf16[128,2048]{1,0:T(8,128)(2,1)}, bf16[128,2048]{1,0:T(8,128)(2,1)}, bf16[1,512,768]{2,1,0:T(8,128)(2,1)}, bf16[1,768,512]{2,1,0:T(8,128)(2,1)}) custom-call(bf16[128,2048]{1,0:T(8,128)(2,1)} %tok.1, bf16[128,2048]{1,0:T(8,128)(2,1)} %cot.1, s32[2,128]{1,0:T(2,128)} %bitcast.2, s32[2,128]{1,0:T(2,128)} %bitcast.3, ...), custom_call_target="tpu_custom_call" | custom-call | tf_op jit(solution)/shard_map/pallas_call | solution.py:445
  68.6 2.6 %shard_map.94 = (bf16[128,2048]{1,0:T(8,128)(2,1)}, bf16[128,2048]{1,0:T(8,128)(2,1)}, bf16[1,512,768]{2,1,0:T(8,128)(2,1)}, bf16[1,768,512]{2,1,0:T(8,128)(2,1)}) custom-call(bf16[128,2048]{1,0:T(8,128)(2,1)} %get-tuple-element.8.refs_0_, bf16[128,2048]{1,0:T(8,128)(2,1)} %get-tuple-element.9.refs_1_, bf16[1,512,768]{2,1,0:T(8,128)(2,1)} %get-tuple-element.10.refs_2_, ...), custom_call_target="tpu_custom_call" | custom-call | tf_op jit(solution)/shard_map/pallas_call | solution.py:510
